TPU v7x, 512 devices: a whole 4x4x16 slice. The times are simulated.
512 devices in a mesh: leaf: 64 (over z, y), sec: 8 (over x, core).
Axes of the slice: x: 4, y: 4, z: 16, core: 2. Of those that a mesh axis runs over, the one named last changes fastest.
Arguments:
- leaf_inv: bfloat16 [524288, 1024], P(('leaf', 'sec')), may hold values from -0.1875 to 0.1875
- subtree_blocks: int32 [64, 8], P('leaf', 'sec'), may hold values from 1 to 8
- subtree_shift_rhs: bfloat16 [524288, 128], P(('leaf', 'sec')), may hold values from -6 to 6
- leaf_noise: bfloat16 [524288, 128], P(('leaf', 'sec')), may hold values from -6 to 6
- leaf_dev: bfloat16 [524288], P(('leaf', 'sec')), may hold values from 0.29882812 to 3
- sep_inv: bfloat16 [16384, 3584], P(('leaf', 'sec')), may hold values from -0.1875 to 0.1875
- sep_panel: bfloat16 [16384, 3584], P(('leaf', 'sec')), may hold values from -0.1875 to 0.1875
- sep_rhs: bfloat16 [3, 16384, 128], P(None, ('leaf', 'sec')), may hold values from -6 to 6
- sep_noise: bfloat16 [3, 16384, 128], P(None, ('leaf', 'sec')), may hold values from -6 to 6
- sep_dev: bfloat16 [3, 16384], P(None, ('leaf', 'sec')), may hold values from 0.29882812 to 3
Outputs:
- subtree_scaled_samples: bfloat16 [524288, 128], P(('leaf', 'sec'))
- sep_sample: bfloat16 [3, 16384, 128], P(None, ('leaf', 'sec'))
All inputs are finite; a program needn't handle non-finite values.
Results may differ from a plain program's by a relative error of at most 0.019.
Values may be sent and summed in bfloat16 or wider, within the bound.
A program may use at most 64 MiB of HBM per device.

v0:
```python
import jax
import jax.numpy as jnp
from jax import lax
from jax.sharding import PartitionSpec as P

BLOCK = 128


def from_partner(block, axis, apart):
    count = lax.axis_size(axis)
    route = []
    for low in range(count):
        high = low | 1 << apart
        if high != low and high < count:
            route += [(low, high), (high, low)]
    return lax.ppermute(block, axis, route)


def pair_gather(block, height):
    leaf_place = lax.axis_index("leaf")
    for bit_index in range(height):
        partner = from_partner(block, "leaf", bit_index)
        upper_half = leaf_place >> bit_index & 1 == 1
        block = jnp.where(
            upper_half, jnp.concatenate([partner, block], 0), jnp.concatenate([block, partner], 0)
        )
    return block


def group_gather(piece, height):
    block = lax.all_gather(piece, "sec", axis=0, tiled=True)
    return pair_gather(block, height)


def halve_pairs(partial_sum, height):
    leaf_place = lax.axis_index("leaf")
    for bit_index in reversed(range(height)):
        half_rows = partial_sum.shape[0] // 2
        lower_rows = partial_sum[:half_rows]
        upper_rows = partial_sum[half_rows:]
        upper_half = leaf_place >> bit_index & 1 == 1
        kept = jnp.where(upper_half, upper_rows, lower_rows)
        outgoing = jnp.where(upper_half, lower_rows, upper_rows)
        partial_sum = kept + from_partner(outgoing, "leaf", bit_index)
    return partial_sum


def group_reduce(partial_sum, height):
    reduced = halve_pairs(partial_sum, height)
    return lax.psum_scatter(reduced, "sec", scatter_dimension=0, tiled=True)


def transposed_product(matrix, vector):
    return lax.dot_general(
        matrix, vector, (((0,), (0,)), ((), ())), preferred_element_type=jnp.float32
    )


def on_device(
    leaf_inv,
    subtree_blocks,
    subtree_shift_rhs,
    leaf_noise,
    leaf_dev,
    sep_inv,
    sep_panel,
    sep_rhs,
    sep_noise,
    sep_dev,
):
    subtree_row_count = leaf_inv.shape[0]
    row_count = sep_inv.shape[0]
    levels = sep_rhs.shape[0]
    sections = lax.axis_size("sec")
    active_rows = subtree_blocks[0, 0] * BLOCK
    row_positions = jnp.arange(subtree_row_count, dtype=jnp.int32)
    row_activity = (row_positions >= subtree_row_count - active_rows)[:, None]
    subtree_shifted = jnp.where(
        row_activity, subtree_shift_rhs, jnp.zeros((), subtree_shift_rhs.dtype)
    )
    forward_subtree = jnp.dot(leaf_inv, subtree_shifted, preferred_element_type=jnp.float32)
    subtree_forward_solution = jnp.where(row_activity, forward_subtree, jnp.float32(0.0)).astype(
        jnp.bfloat16
    )
    top = subtree_forward_solution[subtree_row_count - row_count :]
    solved = []
    for height in range(1, levels + 1):
        span = 2**height * sections * row_count
        offset = (2**height - 2) * sections * row_count
        children = group_gather(top, height)
        panel = sep_panel[:, offset : offset + span]
        inverse_block = sep_inv[:, offset : offset + span]
        reduced = (
            sep_rhs[height - 1].astype(jnp.float32)
            - jnp.dot(panel, children, preferred_element_type=jnp.float32)
        ).astype(jnp.bfloat16)
        whole_reduced = group_gather(reduced, height)
        result = jnp.dot(inverse_block, whole_reduced, preferred_element_type=jnp.float32).astype(
            jnp.bfloat16
        )
        solved.append(result)
        top = result
    samples = [None] * levels
    correction = None
    for height in range(levels, 0, -1):
        span = 2**height * sections * row_count
        offset = (2**height - 2) * sections * row_count
        panel = sep_panel[:, offset : offset + span]
        inverse_block = sep_inv[:, offset : offset + span]
        summed = solved[height - 1].astype(jnp.float32) + sep_noise[height - 1].astype(jnp.float32)
        if correction is not None:
            summed = summed - correction
        vector = summed.astype(jnp.bfloat16)
        backed = group_reduce(transposed_product(inverse_block, vector), height).astype(
            jnp.bfloat16
        )
        samples[height - 1] = (
            sep_dev[height - 1][:, None].astype(jnp.float32) * backed.astype(jnp.float32)
        ).astype(jnp.bfloat16)
        correction = group_reduce(transposed_product(panel, backed), height)
    leading = jnp.zeros((subtree_row_count - row_count, correction.shape[1]), jnp.float32)
    placed = jnp.concatenate([leading, correction], axis=0)
    subtree_summed = (
        subtree_forward_solution.astype(jnp.float32) + leaf_noise.astype(jnp.float32) - placed
    )
    subtree_weight = jnp.where(row_activity, subtree_summed, jnp.float32(0.0)).astype(jnp.bfloat16)
    subtree_solution = transposed_product(leaf_inv, subtree_weight)
    sample_scales = leaf_dev[:, None].astype(jnp.float32)
    subtree_scaled_samples = jnp.where(
        row_activity, sample_scales * subtree_solution, jnp.float32(0.0)
    ).astype(jnp.bfloat16)
    return (subtree_scaled_samples, jnp.stack(samples))


def solution(mesh):
    in_specs = (
        P(("leaf", "sec"), None),
        P("leaf", "sec"),
        P(("leaf", "sec"), None),
        P(("leaf", "sec"), None),
        P(("leaf", "sec")),
        P(("leaf", "sec"), None),
        P(("leaf", "sec"), None),
        P(None, ("leaf", "sec"), None),
        P(None, ("leaf", "sec"), None),
        P(None, ("leaf", "sec")),
    )
    out_specs = (P(("leaf", "sec"), None), P(None, ("leaf", "sec"), None))
    return jax.shard_map(
        on_device, mesh=mesh, in_specs=in_specs, out_specs=out_specs, check_vma=False
    )
```

profile of v0, /device:TPU:8, one launch (start us, length us, event | category | flops | bytes accessed | tf_op | source)
XLA Modules:
  0.0 543.7 jit_solution(11738488947053809435)
XLA Ops:
  10.1 13.1 %all_gather.18 = bf16[256,128]{1,0:T(8,128)(2,1)S(1)} all-gather(bf16[32,128]{1,0:T(8,128)(2,1)S(1)} %copy.28), channel_id=1, replica_groups=mesh['leaf'=64,'sec'=8] {'sec'}, dimensions={0}, use_global_device_ids=true | all-gather | bytes 73728 | tf_op jit(solution)/shard_map/all_gather | solution.py:31
  23.3 7.4 %collective-permute-start = (bf16[256,128]{1,0:T(8,128)(2,1)S(1)}, bf16[256,128]{1,0:T(8,128)(2,1)S(1)}, u32[]{:S(2)}, u32[]{:S(2)}) collective-permute-start(bf16[256,128]{1,0:T(8,128)(2,1)S(1)} %all_gather.18), channel_id=1, source_target_pairs={{0,8},{8,0},{16,24},{24,16},{32,40},{40,32},{48,56},{56,48},{64,72... | collective-permute-start | bytes 196616 | tf_op jit(solution)/shard_map/ppermute | solution.py:16
  33.3 12.7 %all_gather.19 = bf16[256,128]{1,0:T(8,128)(2,1)S(1)} all-gather(bf16[32,128]{1,0:T(8,128)(2,1)S(1)} %fusion.8), channel_id=1, replica_groups=mesh['leaf'=64,'sec'=8] {'sec'}, dimensions={0}, use_global_device_ids=true | all-gather | bytes 73728 | tf_op jit(solution)/shard_map/all_gather | solution.py:31
  53.2 12.7 %all_gather.20 = bf16[256,128]{1,0:T(8,128)(2,1)S(1)} all-gather(bf16[32,128]{1,0:T(8,128)(2,1)S(1)} %fusion.15), channel_id=1, replica_groups=mesh['leaf'=64,'sec'=8] {'sec'}, dimensions={0}, use_global_device_ids=true | all-gather | bytes 73728 | tf_op jit(solution)/shard_map/all_gather | solution.py:31
  74.1 6.4 %collective-permute-done.3 = bf16[512,128]{1,0:T(8,128)(2,1)S(1)} collective-permute-done((bf16[512,128]{1,0:T(8,128)(2,1)S(1)}, bf16[512,128]{1,0:T(8,128)(2,1)S(1)}, u32[]{:S(2)}, u32[]{:S(2)}) %collective-permute-start.3) | collective-permute-done | bytes 131104 | tf_op jit(solution)/shard_map/ppermute | solution.py:16
  80.7 12.8 %all_gather.21 = bf16[256,128]{1,0:T(8,128)(2,1)S(1)} all-gather(bf16[32,128]{1,0:T(8,128)(2,1)S(1)} %fusion.9), channel_id=1, replica_groups=mesh['leaf'=64,'sec'=8] {'sec'}, dimensions={0}, use_global_device_ids=true | all-gather | bytes 73728 | tf_op jit(solution)/shard_map/all_gather | solution.py:31
  101.9 6.2 %collective-permute-done.5 = bf16[512,128]{1,0:T(8,128)(2,1)S(1)} collective-permute-done((bf16[512,128]{1,0:T(8,128)(2,1)S(1)}, bf16[512,128]{1,0:T(8,128)(2,1)S(1)}, u32[]{:S(2)}, u32[]{:S(2)}) %collective-permute-start.5) | collective-permute-done | bytes 131104 | tf_op jit(solution)/shard_map/ppermute | solution.py:16
  109.1 12.8 %all_gather.22 = bf16[256,128]{1,0:T(8,128)(2,1)S(1)} all-gather(bf16[32,128]{1,0:T(8,128)(2,1)S(1)} %fusion.16), channel_id=1, replica_groups=mesh['leaf'=64,'sec'=8] {'sec'}, dimensions={0}, use_global_device_ids=true | all-gather | bytes 73728 | tf_op jit(solution)/shard_map/all_gather | solution.py:31
  130.3 6.2 %collective-permute-done.7 = bf16[512,128]{1,0:T(8,128)(2,1)S(1)} collective-permute-done((bf16[512,128]{1,0:T(8,128)(2,1)S(1)}, bf16[512,128]{1,0:T(8,128)(2,1)S(1)}, u32[]{:S(2)}, u32[]{:S(2)}) %collective-permute-start.7) | collective-permute-done | bytes 131104 | tf_op jit(solution)/shard_map/ppermute | solution.py:16
  138.5 6.5 %collective-permute-done.8 = bf16[1024,128]{1,0:T(8,128)(2,1)S(1)} collective-permute-done((bf16[1024,128]{1,0:T(8,128)(2,1)S(1)}, bf16[1024,128]{1,0:T(8,128)(2,1)S(1)}, u32[]{:S(2)}, u32[]{:S(2)}) %collective-permute-start.8) | collective-permute-done | bytes 262176 | tf_op jit(solution)/shard_map/ppermute | solution.py:16
  145.3 12.8 %all_gather.23 = bf16[256,128]{1,0:T(8,128)(2,1)S(1)} all-gather(bf16[32,128]{1,0:T(8,128)(2,1)S(1)} %fusion.10), channel_id=1, replica_groups=mesh['leaf'=64,'sec'=8] {'sec'}, dimensions={0}, use_global_device_ids=true | all-gather | bytes 73728 | tf_op jit(solution)/shard_map/all_gather | solution.py:31
  166.5 6.2 %collective-permute-done.10 = bf16[512,128]{1,0:T(8,128)(2,1)S(1)} collective-permute-done((bf16[512,128]{1,0:T(8,128)(2,1)S(1)}, bf16[512,128]{1,0:T(8,128)(2,1)S(1)}, u32[]{:S(2)}, u32[]{:S(2)}) %collective-permute-start.10) | collective-permute-done | bytes 131104 | tf_op jit(solution)/shard_map/ppermute | solution.py:16
  175.0 6.4 %collective-permute-done.11 = bf16[1024,128]{1,0:T(8,128)(2,1)} collective-permute-done((bf16[1024,128]{1,0:T(8,128)(2,1)S(1)}, bf16[1024,128]{1,0:T(8,128)(2,1)}, u32[]{:S(2)}, u32[]{:S(2)}) %collective-permute-start.11) | collective-permute-done | bytes 262176 | tf_op jit(solution)/shard_map/ppermute | solution.py:16
  185.5 11.0 %collective-permute-done.12 = f32[1024,128]{0,1:T(8,128)S(1)} collective-permute-done((f32[1024,128]{0,1:T(8,128)S(1)}, f32[1024,128]{0,1:T(8,128)S(1)}, u32[]{:S(2)}, u32[]{:S(2)}) %collective-permute-start.12) | collective-permute-done | bytes 524320 | tf_op jit(solution)/shard_map/ppermute | solution.py:16
  198.9 8.2 %collective-permute-done.13 = f32[512,128]{0,1:T(8,128)S(1)} collective-permute-done((f32[512,128]{0,1:T(8,128)S(1)}, f32[512,128]{0,1:T(8,128)S(1)}, u32[]{:S(2)}, u32[]{:S(2)}) %collective-permute-start.13) | collective-permute-done | bytes 262176 | tf_op jit(solution)/shard_map/ppermute | solution.py:16
  214.9 37.6 %reduce-scatter.19.cloned.1.call-done = f32[32,128]{1,0:T(8,128)} async-done(((f32[256,128]{1,0:T(8,128)}), f32[32,128]{1,0:T(8,128)}) %reduce-scatter.19.cloned.1.call-update) | async-done | bytes 16400
  257.3 9.5 %collective-permute-done.15 = f32[1024,128]{0,1:T(8,128)S(1)} collective-permute-done((f32[1024,128]{0,1:T(8,128)S(1)}, f32[1024,128]{0,1:T(8,128)S(1)}, u32[]{:S(2)}, u32[]{:S(2)}) %collective-permute-start.15) | collective-permute-done | bytes 524320 | tf_op jit(solution)/shard_map/ppermute | solution.py:16
  266.9 4.1 collective-permute-start.16
  271.0 5.7 %collective-permute-done.16 = f32[512,128]{0,1:T(8,128)S(1)} collective-permute-done((f32[512,128]{0,1:T(8,128)S(1)}, f32[512,128]{0,1:T(8,128)S(1)}, u32[]{:S(2)}, u32[]{:S(2)}) %collective-permute-start.16) | collective-permute-done | bytes 262176 | tf_op jit(solution)/shard_map/ppermute | solution.py:16
  284.5 41.8 %reduce-scatter.21.cloned.1.call-done = f32[32,128]{1,0:T(8,128)} async-done(((f32[256,128]{1,0:T(8,128)}), f32[32,128]{1,0:T(8,128)}) %reduce-scatter.21.cloned.1.call-update) | async-done | bytes 16400 | tf_op jit(solution)/shard_map/reduce_scatter | solution.py:50
  327.4 4.0 collective-permute-start.18
  331.4 5.8 %collective-permute-done.18 = f32[512,128]{0,1:T(8,128)S(1)} collective-permute-done((f32[512,128]{0,1:T(8,128)S(1)}, f32[512,128]{0,1:T(8,128)S(1)}, u32[]{:S(2)}, u32[]{:S(2)}) %collective-permute-start.18) | collective-permute-done | bytes 262176 | tf_op jit(solution)/shard_map/ppermute | solution.py:16
  339.8 4.3 collective-permute-done.19
  344.9 39.3 %reduce-scatter.23.cloned.1.call-done = f32[32,128]{1,0:T(8,128)} async-done(((f32[256,128]{1,0:T(8,128)}), f32[32,128]{1,0:T(8,128)}) %reduce-scatter.23.cloned.1.call-update) | async-done | bytes 16400
  385.4 4.2 collective-permute-start.20
  389.6 5.7 %collective-permute-done.20 = f32[512,128]{0,1:T(8,128)S(1)} collective-permute-done((f32[512,128]{0,1:T(8,128)S(1)}, f32[512,128]{0,1:T(8,128)S(1)}, u32[]{:S(2)}, u32[]{:S(2)}) %collective-permute-start.20) | collective-permute-done | bytes 262176 | tf_op jit(solution)/shard_map/ppermute | solution.py:16
  397.9 4.3 collective-permute-done.21
  403.1 39.4 %reduce-scatter.25.cloned.1.call-done = f32[32,128]{1,0:T(8,128)} async-done(((f32[256,128]{1,0:T(8,128)}), f32[32,128]{1,0:T(8,128)}) %reduce-scatter.25.cloned.1.call-update) | async-done | bytes 16400 | tf_op jit(solution)/shard_map/reduce_scatter | solution.py:50
  446.0 4.4 collective-permute-done.22
  451.5 37.2 %reduce-scatter.27.cloned.1.call-done = f32[32,128]{1,0:T(8,128)} async-done(((f32[256,128]{1,0:T(8,128)}), f32[32,128]{1,0:T(8,128)}) %reduce-scatter.27.cloned.1.call-update) | async-done | bytes 16400
  492.3 4.3 collective-permute-done.23
  498.1 36.7 %reduce-scatter.29.cloned.1.call-done = f32[32,128]{1,0:T(8,128)} async-done(((f32[256,128]{1,0:T(8,128)}), f32[32,128]{1,0:T(8,128)}) %reduce-scatter.29.cloned.1.call-update) | async-done | bytes 16400
  (126 shorter events, 98.8 us)
Async XLA Ops:
  7.2 245.3 %reduce-scatter.19.cloned.1.call-start = ((), (), s32[]{:S(2)}) async-start(), calls=%async_computation.6 | async-start | bytes 147456
  23.3 9.9 %collective-permute-start = (bf16[256,128]{1,0:T(8,128)(2,1)S(1)}, bf16[256,128]{1,0:T(8,128)(2,1)S(1)}, u32[]{:S(2)}, u32[]{:S(2)}) collective-permute-start(bf16[256,128]{1,0:T(8,128)(2,1)S(1)} %all_gather.18), channel_id=1, source_target_pairs={{0,8},{8,0},{16,24},{24,16},{32,40},{40,32},{48,56},{56,48},{64,72... | collective-permute-start | bytes 196616 | tf_op jit(solution)/shard_map/ppermute | solution.py:16
  46.1 6.2 %collective-permute-start.1 = (bf16[256,128]{1,0:T(8,128)(2,1)S(1)}, bf16[256,128]{1,0:T(8,128)(2,1)S(1)}, u32[]{:S(2)}, u32[]{:S(2)}) collective-permute-start(bf16[256,128]{1,0:T(8,128)(2,1)S(1)} %all_gather.19), channel_id=1, source_target_pairs={{0,8},{8,0},{16,24},{24,16},{32,40},{40,32},{48,56},{56,48},{64,72... | collective-permute-start | bytes 196616 | tf_op jit(solution)/shard_map/ppermute | solution.py:16
  65.9 6.2 %collective-permute-start.2 = (bf16[256,128]{1,0:T(8,128)(2,1)S(1)}, bf16[256,128]{1,0:T(8,128)(2,1)S(1)}, u32[]{:S(2)}, u32[]{:S(2)}) collective-permute-start(bf16[256,128]{1,0:T(8,128)(2,1)S(1)} %all_gather.20), channel_id=1, source_target_pairs={{0,8},{8,0},{16,24},{24,16},{32,40},{40,32},{48,56},{56,48},{64,72... | collective-permute-start | bytes 196616 | tf_op jit(solution)/shard_map/ppermute | solution.py:16
  72.2 8.4 %collective-permute-start.3 = (bf16[512,128]{1,0:T(8,128)(2,1)S(1)}, bf16[512,128]{1,0:T(8,128)(2,1)S(1)}, u32[]{:S(2)}, u32[]{:S(2)}) collective-permute-start(bf16[512,128]{1,0:T(8,128)(2,1)S(1)} %maximum_select_fusion.15), channel_id=1, source_target_pairs={{0,16},{16,0},{8,24},{24,8},{32,48},{48,32},{40,56},{56,40},{64,80... | collective-permute-start | bytes 393224 | tf_op jit(solution)/shard_map/ppermute | solution.py:16
  93.5 6.2 %collective-permute-start.4 = (bf16[256,128]{1,0:T(8,128)(2,1)S(1)}, bf16[256,128]{1,0:T(8,128)(2,1)S(1)}, u32[]{:S(2)}, u32[]{:S(2)}) collective-permute-start(bf16[256,128]{1,0:T(8,128)(2,1)S(1)} %all_gather.21), channel_id=1, source_target_pairs={{0,8},{8,0},{16,24},{24,16},{32,40},{40,32},{48,56},{56,48},{64,72... | collective-permute-start | bytes 196616 | tf_op jit(solution)/shard_map/ppermute | solution.py:16
  99.7 8.4 %collective-permute-start.5 = (bf16[512,128]{1,0:T(8,128)(2,1)S(1)}, bf16[512,128]{1,0:T(8,128)(2,1)S(1)}, u32[]{:S(2)}, u32[]{:S(2)}) collective-permute-start(bf16[512,128]{1,0:T(8,128)(2,1)S(1)} %maximum_select_fusion.16), channel_id=1, source_target_pairs={{0,16},{16,0},{8,24},{24,8},{32,48},{48,32},{40,56},{56,40},{64,80... | collective-permute-start | bytes 393224 | tf_op jit(solution)/shard_map/ppermute | solution.py:16
  109.1 72.2 %copy-start.5 = (bf16[3,32,128]{2,1,0:T(8,128)(2,1)S(1)}, bf16[3,32,128]{2,1,0:T(8,128)(2,1)}, u32[]{:S(2)}) copy-start(bf16[3,32,128]{2,1,0:T(8,128)(2,1)} %param.18) | copy-start | bytes 73732
  121.9 6.2 %collective-permute-start.6 = (bf16[256,128]{1,0:T(8,128)(2,1)S(1)}, bf16[256,128]{1,0:T(8,128)(2,1)S(1)}, u32[]{:S(2)}, u32[]{:S(2)}) collective-permute-start(bf16[256,128]{1,0:T(8,128)(2,1)S(1)} %all_gather.22), channel_id=1, source_target_pairs={{0,8},{8,0},{16,24},{24,16},{32,40},{40,32},{48,56},{56,48},{64,72... | collective-permute-start | bytes 196616 | tf_op jit(solution)/shard_map/ppermute | solution.py:16
  128.1 8.4 %collective-permute-start.7 = (bf16[512,128]{1,0:T(8,128)(2,1)S(1)}, bf16[512,128]{1,0:T(8,128)(2,1)S(1)}, u32[]{:S(2)}, u32[]{:S(2)}) collective-permute-start(bf16[512,128]{1,0:T(8,128)(2,1)S(1)} %maximum_select_fusion.17), channel_id=1, source_target_pairs={{0,16},{16,0},{8,24},{24,8},{32,48},{48,32},{40,56},{56,40},{64,80... | collective-permute-start | bytes 393224 | tf_op jit(solution)/shard_map/ppermute | solution.py:16
  136.6 8.5 %collective-permute-start.8 = (bf16[1024,128]{1,0:T(8,128)(2,1)S(1)}, bf16[1024,128]{1,0:T(8,128)(2,1)S(1)}, u32[]{:S(2)}, u32[]{:S(2)}) collective-permute-start(bf16[1024,128]{1,0:T(8,128)(2,1)S(1)} %maximum_select_fusion.9), channel_id=1, source_target_pairs={{0,32},{32,0},{8,40},{40,8},{16,48},{48,16},{24,56},{56,24},{64,96... | collective-permute-start | bytes 786440 | tf_op jit(solution)/shard_map/ppermute | solution.py:16
  158.0 6.2 %collective-permute-start.9 = (bf16[256,128]{1,0:T(8,128)(2,1)S(1)}, bf16[256,128]{1,0:T(8,128)(2,1)S(1)}, u32[]{:S(2)}, u32[]{:S(2)}) collective-permute-start(bf16[256,128]{1,0:T(8,128)(2,1)S(1)} %all_gather.23), channel_id=1, source_target_pairs={{0,8},{8,0},{16,24},{24,16},{32,40},{40,32},{48,56},{56,48},{64,72... | collective-permute-start | bytes 196616 | tf_op jit(solution)/shard_map/ppermute | solution.py:16
  164.3 8.4 %collective-permute-start.10 = (bf16[512,128]{1,0:T(8,128)(2,1)S(1)}, bf16[512,128]{1,0:T(8,128)(2,1)S(1)}, u32[]{:S(2)}, u32[]{:S(2)}) collective-permute-start(bf16[512,128]{1,0:T(8,128)(2,1)S(1)} %maximum_select_fusion.18), channel_id=1, source_target_pairs={{0,16},{16,0},{8,24},{24,8},{32,48},{48,32},{40,56},{56,40},{64,80... | collective-permute-start | bytes 393224 | tf_op jit(solution)/shard_map/ppermute | solution.py:16
  172.7 8.6 %collective-permute-start.11 = (bf16[1024,128]{1,0:T(8,128)(2,1)S(1)}, bf16[1024,128]{1,0:T(8,128)(2,1)}, u32[]{:S(2)}, u32[]{:S(2)}) collective-permute-start(bf16[1024,128]{1,0:T(8,128)(2,1)S(1)} %maximum_select_fusion.10), channel_id=1, source_target_pairs={{0,32},{32,0},{8,40},{40,8},{16,48},{48,16},{24,56},{56,24},{64,96... | collective-permute-start | bytes 786440 | tf_op jit(solution)/shard_map/ppermute | solution.py:16
  183.3 13.2 %collective-permute-start.12 = (f32[1024,128]{0,1:T(8,128)S(1)}, f32[1024,128]{0,1:T(8,128)S(1)}, u32[]{:S(2)}, u32[]{:S(2)}) collective-permute-start(f32[1024,128]{0,1:T(8,128)S(1)} %slice_select_fusion.1), channel_id=1, source_target_pairs={{0,32},{32,0},{8,40},{40,8},{16,48},{48,16},{24,56},{56,24},{64,96... | collective-permute-start | bytes 1572872 | tf_op jit(solution)/shard_map/ppermute | solution.py:16
  196.6 10.5 %collective-permute-start.13 = (f32[512,128]{0,1:T(8,128)S(1)}, f32[512,128]{0,1:T(8,128)S(1)}, u32[]{:S(2)}, u32[]{:S(2)}) collective-permute-start(f32[512,128]{0,1:T(8,128)S(1)} %slice_select_fusion.5), channel_id=1, source_target_pairs={{0,16},{16,0},{8,24},{24,8},{32,48},{48,32},{40,56},{56,40},{64,80... | collective-permute-start | bytes 786440 | tf_op jit(solution)/shard_map/ppermute | solution.py:16
  207.2 6.9 %collective-permute-start.14 = (f32[256,128]{0,1:T(8,128)S(1)}, f32[256,128]{0,1:T(8,128)S(1)}, u32[]{:S(2)}, u32[]{:S(2)}) collective-permute-start(f32[256,128]{0,1:T(8,128)S(1)} %slice_select_fusion.11), channel_id=1, source_target_pairs={{0,8},{8,0},{16,24},{24,16},{32,40},{40,32},{48,56},{56,48},{64,72... | collective-permute-start | bytes 393224 | tf_op jit(solution)/shard_map/ppermute | solution.py:16
  214.8 111.4 %reduce-scatter.21.cloned.1.call-start = ((), (), s32[]{:S(2)}) async-start(), calls=%async_computation.7 | async-start | bytes 147456 | tf_op jit(solution)/shard_map/reduce_scatter | solution.py:50
  253.7 13.1 %collective-permute-start.15 = (f32[1024,128]{0,1:T(8,128)S(1)}, f32[1024,128]{0,1:T(8,128)S(1)}, u32[]{:S(2)}, u32[]{:S(2)}) collective-permute-start(f32[1024,128]{0,1:T(8,128)S(1)} %slice_select_fusion), channel_id=1, source_target_pairs={{0,32},{32,0},{8,40},{40,8},{16,48},{48,16},{24,56},{56,24},{64,96... | collective-permute-start | bytes 1572872 | tf_op jit(solution)/shard_map/ppermute | solution.py:16
  266.9 9.8 %collective-permute-start.16 = (f32[512,128]{0,1:T(8,128)S(1)}, f32[512,128]{0,1:T(8,128)S(1)}, u32[]{:S(2)}, u32[]{:S(2)}) collective-permute-start(f32[512,128]{0,1:T(8,128)S(1)} %slice_select_fusion.4), channel_id=1, source_target_pairs={{0,16},{16,0},{8,24},{24,8},{32,48},{48,32},{40,56},{56,40},{64,80... | collective-permute-start | bytes 786440 | tf_op jit(solution)/shard_map/ppermute | solution.py:16
  276.7 6.9 %collective-permute-start.17 = (f32[256,128]{0,1:T(8,128)S(1)}, f32[256,128]{0,1:T(8,128)S(1)}, u32[]{:S(2)}, u32[]{:S(2)}) collective-permute-start(f32[256,128]{0,1:T(8,128)S(1)} %slice_select_fusion.10), channel_id=1, source_target_pairs={{0,8},{8,0},{16,24},{24,16},{32,40},{40,32},{48,56},{56,48},{64,72... | collective-permute-start | bytes 393224 | tf_op jit(solution)/shard_map/ppermute | solution.py:16
  284.4 99.9 %reduce-scatter.23.cloned.1.call-start = ((), (), s32[]{:S(2)}) async-start(), calls=%async_computation.8 | async-start | bytes 147456
  327.4 9.8 %collective-permute-start.18 = (f32[512,128]{0,1:T(8,128)S(1)}, f32[512,128]{0,1:T(8,128)S(1)}, u32[]{:S(2)}, u32[]{:S(2)}) collective-permute-start(f32[512,128]{0,1:T(8,128)S(1)} %slice_select_fusion.3), channel_id=1, source_target_pairs={{0,16},{16,0},{8,24},{24,8},{32,48},{48,32},{40,56},{56,40},{64,80... | collective-permute-start | bytes 786440 | tf_op jit(solution)/shard_map/ppermute | solution.py:16
  337.2 6.9 %collective-permute-start.19 = (f32[256,128]{0,1:T(8,128)S(1)}, f32[256,128]{0,1:T(8,128)S(1)}, u32[]{:S(2)}, u32[]{:S(2)}) collective-permute-start(f32[256,128]{0,1:T(8,128)S(1)} %slice_select_fusion.9), channel_id=1, source_target_pairs={{0,8},{8,0},{16,24},{24,16},{32,40},{40,32},{48,56},{56,48},{64,72... | collective-permute-start | bytes 393224 | tf_op jit(solution)/shard_map/ppermute | solution.py:16
  344.9 97.6 %reduce-scatter.25.cloned.1.call-start = ((), (), s32[]{:S(2)}) async-start(), calls=%async_computation.9 | async-start | bytes 147456 | tf_op jit(solution)/shard_map/reduce_scatter | solution.py:50
  385.4 66.1 %copy-start.7 = (bf16[1024]{0:T(1024)(128)(2,1)S(1)}, bf16[1024]{0:T(1024)(128)(2,1)}, u32[]{:S(2)}) copy-start(bf16[1024]{0:T(1024)(128)(2,1)} %param.14) | copy-start | bytes 6148
  385.4 9.9 %collective-permute-start.20 = (f32[512,128]{0,1:T(8,128)S(1)}, f32[512,128]{0,1:T(8,128)S(1)}, u32[]{:S(2)}, u32[]{:S(2)}) collective-permute-start(f32[512,128]{0,1:T(8,128)S(1)} %slice_select_fusion.2), channel_id=1, source_target_pairs={{0,16},{16,0},{8,24},{24,8},{32,48},{48,32},{40,56},{56,40},{64,80... | collective-permute-start | bytes 786440 | tf_op jit(solution)/shard_map/ppermute | solution.py:16
  395.4 6.9 %collective-permute-start.21 = (f32[256,128]{0,1:T(8,128)S(1)}, f32[256,128]{0,1:T(8,128)S(1)}, u32[]{:S(2)}, u32[]{:S(2)}) collective-permute-start(f32[256,128]{0,1:T(8,128)S(1)} %slice_select_fusion.8), channel_id=1, source_target_pairs={{0,8},{8,0},{16,24},{24,16},{32,40},{40,32},{48,56},{56,48},{64,72... | collective-permute-start | bytes 393224 | tf_op jit(solution)/shard_map/ppermute | solution.py:16
  403.0 85.7 %reduce-scatter.27.cloned.1.call-start = ((), (), s32[]{:S(2)}) async-start(), calls=%async_computation.10 | async-start | bytes 147456
  443.5 6.9 %collective-permute-start.22 = (f32[256,128]{0,1:T(8,128)S(1)}, f32[256,128]{0,1:T(8,128)S(1)}, u32[]{:S(2)}, u32[]{:S(2)}) collective-permute-start(f32[256,128]{0,1:T(8,128)S(1)} %slice_select_fusion.7), channel_id=1, source_target_pairs={{0,8},{8,0},{16,24},{24,16},{32,40},{40,32},{48,56},{56,48},{64,72... | collective-permute-start | bytes 393224 | tf_op jit(solution)/shard_map/ppermute | solution.py:16
  451.2 83.6 %reduce-scatter.29.cloned.1.call-start = ((), (), s32[]{:S(2)}) async-start(), calls=%async_computation.11 | async-start | bytes 147456
  489.7 6.9 %collective-permute-start.23 = (f32[256,128]{0,1:T(8,128)S(1)}, f32[256,128]{0,1:T(8,128)S(1)}, u32[]{:S(2)}, u32[]{:S(2)}) collective-permute-start(f32[256,128]{0,1:T(8,128)S(1)} %slice_select_fusion.6), channel_id=1, source_target_pairs={{0,8},{8,0},{16,24},{24,16},{32,40},{40,32},{48,56},{56,48},{64,72... | collective-permute-start | bytes 393224 | tf_op jit(solution)/shard_map/ppermute | solution.py:16
  (7 other events, 244.9 us)
Sparse Core Ops, SparseCore 0:
  215.0 37.4 reduce-scatter.18
  284.5 41.6 reduce-scatter.20
  345.0 39.2 reduce-scatter.22
  403.1 39.3 reduce-scatter.24
  451.3 37.3 reduce-scatter.26
  497.5 37.2 reduce-scatter.28
where the time goes:
time: 545 us; the launch traced here: 544 us
  waiting for transfers between devices  355 us (65%)
  blocking collectives  76.8 us (14%)
  starting transfers between devices  76.1 us (14%)
  between operations  15.5 us (3%)
  local copies, waits for them, and re-layouts  10.3 us (2%)
  matrix products  8.35 us (2%)
    unnamed x10, waiting for transfers between devices  151 us
    ppermute x24, waiting for transfers between devices, from_partner(): return lax.ppermute(block, axis, route)  123 us
    reduce_scatter x2, waiting for transfers between devices, group_reduce(): return lax.psum_scatter(reduced, 'sec', scatter_dimension=0, tiled=True)  81.2 us
    all_gather x6, blocking collectives, group_gather(): block = lax.all_gather(piece, 'sec', axis=0, tiled=True)  76.8 us
    ppermute x24, starting transfers between devices, from_partner(): return lax.ppermute(block, axis, route)  75.9 us
  transfers between devices with their start and end apart: 30, of which 30 were waited for; matrix products, arithmetic and copies ran while one was open for 0% of the time, Pallas kernels for 0%

commit v1 on v0

--- a/solution.py
+++ b/solution.py
@@ -4,6 +4,30 @@
 from jax.sharding import PartitionSpec as P
 
 BLOCK = 128
+
+
+def _perform_links(array_in, ax_name="sec"):
+    extra, earlier, res = (lax.axis_size(ax_name), lax.axis_index(ax_name), array_in.shape[0])
+    rows = [to_i * extra if t == 0 else to_i for t, to_i in enumerate(array_in.shape)]
+    vec_out = lax.dynamic_update_slice_in_dim(
+        jnp.zeros(rows, array_in.dtype), array_in, earlier * res, axis=0
+    )
+    s_next = clean = array_in
+    for m in range(1, extra // 2 + 1):
+        s_next = lax.ppermute(
+            s_next, axis_name=ax_name, perm=list(map(lambda t: (t, (t + 1) % extra), range(extra)))
+        )
+        vec_out = lax.dynamic_update_slice_in_dim(
+            vec_out, s_next, (earlier - m) % extra * res, axis=0
+        )
+        if 2 * m < extra:
+            clean = lax.ppermute(
+                clean, ax_name, perm=list(map(lambda t: (t, (t - 1) % extra), range(extra)))
+            )
+            vec_out = lax.dynamic_update_slice_in_dim(
+                vec_out, clean, (earlier + m) % extra * res, axis=0
+            )
+    return vec_out
 
 
 def from_partner(block, axis, apart):
@@ -28,7 +52,7 @@
 
 
 def group_gather(piece, height):
-    block = lax.all_gather(piece, "sec", axis=0, tiled=True)
+    block = _perform_links(piece)
     return pair_gather(block, height)
 
 

time: 545 us -> 578 us (1.061)
  blocking collectives: 76.8 us -> 0 us
  starting transfers between devices: 76.1 us -> 132 us
  waiting for transfers between devices: 355 us -> 386 us
  local copies, waits for them, and re-layouts: 10.3 us -> 32.6 us
    all_gather x6 -> x0, blocking collectives: 76.8 us -> none  [group_gather(): block = lax.all_gather(piece, 'sec', axis=0, tiled=True)]
    ppermute x0 -> x42, starting transfers between devices: none -> 53 us  [the longest x18 52.8 us: _perform_links(): lax.ppermute(clean, ax_name, perm=list(map(lambda t: (t, (t - 1) % extra)...]
    ppermute x0 -> x42, waiting for transfers between devices: none -> 29.9 us  [the longest x24 29.6 us: _perform_links(): lax.ppermute(s_next, axis_name=ax_name, perm=list(map(lambda t: (t, (t +...]
    dynamic_update_slice x0 -> x48, local copies, waits for them, and re-layouts: none -> 17.5 us  [the longest x24 8.39 us: _perform_links(): lax.dynamic_update_slice_in_dim(vec_out, s_next, (earlier - m) % extra *...]
  transfers between devices with their start and end apart: 30 -> 72, of which waited for: 30 -> 54; matrix products, arithmetic and copies ran while one was open for 0% -> 4% of each run, Pallas kernels for 0% -> 0%
where the time goes in v1:
time: 578 us; the launch traced here: 577 us
  waiting for transfers between devices  386 us (67%)
  starting transfers between devices  132 us (23%)
  local copies, waits for them, and re-layouts  32.6 us (6%)
  between operations  16.1 us (3%)
  matrix products  8.47 us (1%)
    unnamed x10, waiting for transfers between devices  155 us
    ppermute x24, waiting for transfers between devices, from_partner(): return lax.ppermute(block, axis, route)  120 us
    reduce_scatter x2, waiting for transfers between devices, group_reduce(): return lax.psum_scatter(reduced, 'sec', scatter_dimension=0, tiled=True)  81.1 us
    ppermute x24, starting transfers between devices, from_partner(): return lax.ppermute(block, axis, route)  78.5 us
    ppermute x18, starting transfers between devices, _perform_links(): lax.ppermute(clean, ax_name, perm=list(map(lambda t: (t, (t - 1) % extra)...  52.8 us
    ppermute x24, waiting for transfers between devices, _perform_links(): lax.ppermute(s_next, axis_name=ax_name, perm=list(map(lambda t: (t, (t +...  29.6 us
  transfers between devices with their start and end apart: 72, of which 54 were waited for; matrix products, arithmetic and copies ran while one was open for 4% of the time, Pallas kernels for 0%

profile of v1, /device:TPU:8, one launch (start us, length us, event | category | flops | bytes accessed | tf_op | source)
XLA Modules:
  0.0 576.9 jit_solution(15865627466089217905)
XLA Ops:
  28.5 7.7 %collective-permute-start.7 = (bf16[256,128]{0,1:T(8,128)(2,1)S(1)}, bf16[256,128]{0,1:T(8,128)(2,1)S(1)}, u32[]{:S(2)}, u32[]{:S(2)}) collective-permute-start(bf16[256,128]{0,1:T(8,128)(2,1)S(1)} %dynamic_update_slice.151), channel_id=1, source_target_pairs={{0,8},{8,0},{16,24},{24,16},{32,40},{40,32},{48,56},{56,48},{64,72... | collective-permute-start | bytes 196616 | tf_op jit(solution)/shard_map/ppermute | solution.py:40
  56.1 3.9 collective-permute-start.15
  80.6 3.9 collective-permute-start.23
  89.2 6.3 %collective-permute-done.24 = bf16[512,128]{0,1:T(8,128)(2,1)S(1)} collective-permute-done((bf16[512,128]{0,1:T(8,128)(2,1)S(1)}, bf16[512,128]{0,1:T(8,128)(2,1)S(1)}, u32[]{:S(2)}, u32[]{:S(2)}) %collective-permute-start.24) | collective-permute-done | bytes 131104 | tf_op jit(solution)/shard_map/ppermute | solution.py:40
  113.1 4.4 collective-permute-start.32
  121.9 6.4 %collective-permute-done.33 = bf16[512,128]{0,1:T(8,128)(2,1)S(1)} collective-permute-done((bf16[512,128]{0,1:T(8,128)(2,1)S(1)}, bf16[512,128]{0,1:T(8,128)(2,1)S(1)}, u32[]{:S(2)}, u32[]{:S(2)}) %collective-permute-start.33) | collective-permute-done | bytes 131104 | tf_op jit(solution)/shard_map/ppermute | solution.py:40
  146.9 4.4 collective-permute-start.41
  155.7 6.4 %collective-permute-done.42 = bf16[512,128]{0,1:T(8,128)(2,1)S(1)} collective-permute-done((bf16[512,128]{0,1:T(8,128)(2,1)S(1)}, bf16[512,128]{0,1:T(8,128)(2,1)S(1)}, u32[]{:S(2)}, u32[]{:S(2)}) %collective-permute-start.42) | collective-permute-done | bytes 131104 | tf_op jit(solution)/shard_map/ppermute | solution.py:40
  164.2 6.3 %collective-permute-done.43 = bf16[1024,128]{0,1:T(8,128)(2,1)S(1)} collective-permute-done((bf16[1024,128]{0,1:T(8,128)(2,1)S(1)}, bf16[1024,128]{0,1:T(8,128)(2,1)S(1)}, u32[]{:S(2)}, u32[]{:S(2)}) %collective-permute-start.43) | collective-permute-done | bytes 262176 | tf_op jit(solution)/shard_map/ppermute | solution.py:40
  188.3 4.4 collective-permute-start.51
  197.1 6.4 %collective-permute-done.52 = bf16[512,128]{0,1:T(8,128)(2,1)S(1)} collective-permute-done((bf16[512,128]{0,1:T(8,128)(2,1)S(1)}, bf16[512,128]{0,1:T(8,128)(2,1)S(1)}, u32[]{:S(2)}, u32[]{:S(2)}) %collective-permute-start.52) | collective-permute-done | bytes 131104 | tf_op jit(solution)/shard_map/ppermute | solution.py:40
  205.6 6.4 %collective-permute-done.53 = bf16[1024,128]{0,1:T(8,128)(2,1)} collective-permute-done((bf16[1024,128]{0,1:T(8,128)(2,1)S(1)}, bf16[1024,128]{0,1:T(8,128)(2,1)}, u32[]{:S(2)}, u32[]{:S(2)}) %collective-permute-start.53) | collective-permute-done | bytes 262176 | tf_op jit(solution)/shard_map/ppermute | solution.py:40
  216.0 9.1 %collective-permute-done.54 = f32[1024,128]{0,1:T(8,128)S(1)} collective-permute-done((f32[1024,128]{0,1:T(8,128)S(1)}, f32[1024,128]{0,1:T(8,128)S(1)}, u32[]{:S(2)}, u32[]{:S(2)}) %collective-permute-start.54) | collective-permute-done | bytes 524320 | tf_op jit(solution)/shard_map/ppermute | solution.py:40
  227.3 7.8 %collective-permute-done.55 = f32[512,128]{0,1:T(8,128)S(1)} collective-permute-done((f32[512,128]{0,1:T(8,128)S(1)}, f32[512,128]{0,1:T(8,128)S(1)}, u32[]{:S(2)}, u32[]{:S(2)}) %collective-permute-start.55) | collective-permute-done | bytes 262176 | tf_op jit(solution)/shard_map/ppermute | solution.py:40
  235.2 4.7 collective-permute-start.56
  243.8 41.8 %reduce-scatter.19.cloned.1.call-done = f32[32,128]{1,0:T(8,128)} async-done(((f32[256,128]{1,0:T(8,128)}), f32[32,128]{1,0:T(8,128)}) %reduce-scatter.19.cloned.1.call-update) | async-done | bytes 16400
  290.5 9.3 %collective-permute-done.57 = f32[1024,128]{0,1:T(8,128)S(1)} collective-permute-done((f32[1024,128]{0,1:T(8,128)S(1)}, f32[1024,128]{0,1:T(8,128)S(1)}, u32[]{:S(2)}, u32[]{:S(2)}) %collective-permute-start.57) | collective-permute-done | bytes 524320 | tf_op jit(solution)/shard_map/ppermute | solution.py:40
  299.9 4.0 collective-permute-start.58
  304.0 5.7 collective-permute-done.58
  317.5 41.7 %reduce-scatter.21.cloned.1.call-done = f32[32,128]{1,0:T(8,128)} async-done(((f32[256,128]{1,0:T(8,128)}), f32[32,128]{1,0:T(8,128)}) %reduce-scatter.21.cloned.1.call-update) | async-done | bytes 16400 | tf_op jit(solution)/shard_map/reduce_scatter | solution.py:74
  360.4 4.0 collective-permute-start.60
  364.4 5.8 collective-permute-done.60
  372.8 4.3 collective-permute-done.61
  378.0 39.4 %reduce-scatter.23.cloned.1.call-done = f32[32,128]{1,0:T(8,128)} async-done(((f32[256,128]{1,0:T(8,128)}), f32[32,128]{1,0:T(8,128)}) %reduce-scatter.23.cloned.1.call-update) | async-done | bytes 16400
  418.5 4.1 collective-permute-start.62
  422.6 5.8 %collective-permute-done.62 = f32[512,128]{0,1:T(8,128)S(1)} collective-permute-done((f32[512,128]{0,1:T(8,128)S(1)}, f32[512,128]{0,1:T(8,128)S(1)}, u32[]{:S(2)}, u32[]{:S(2)}) %collective-permute-start.62) | collective-permute-done | bytes 262176 | tf_op jit(solution)/shard_map/ppermute | solution.py:40
  431.1 4.3 collective-permute-done.63
  436.2 39.4 %reduce-scatter.25.cloned.1.call-done = f32[32,128]{1,0:T(8,128)} async-done(((f32[256,128]{1,0:T(8,128)}), f32[32,128]{1,0:T(8,128)}) %reduce-scatter.25.cloned.1.call-update) | async-done | bytes 16400 | tf_op jit(solution)/shard_map/reduce_scatter | solution.py:74
  479.1 4.4 collective-permute-done.64
  484.6 37.0 %reduce-scatter.27.cloned.1.call-done = f32[32,128]{1,0:T(8,128)} async-done(((f32[256,128]{1,0:T(8,128)}), f32[32,128]{1,0:T(8,128)}) %reduce-scatter.27.cloned.1.call-update) | async-done | bytes 16400
  525.2 4.3 collective-permute-done.65
  531.0 36.9 %reduce-scatter.29.cloned.1.call-done = f32[32,128]{1,0:T(8,128)} async-done(((f32[256,128]{1,0:T(8,128)}), f32[32,128]{1,0:T(8,128)}) %reduce-scatter.29.cloned.1.call-update) | async-done | bytes 16400
  (297 shorter events, 179.8 us)
Async XLA Ops:
  7.2 278.4 %reduce-scatter.19.cloned.1.call-start = ((), (), s32[]{:S(2)}) async-start(), calls=%async_computation.6 | async-start | bytes 147456
  19.2 7.0 %collective-permute-start.5 = (bf16[32,128]{0,1:T(8,128)(2,1)S(1)}, bf16[32,128]{0,1:T(8,128)(2,1)S(1)}, u32[]{:S(2)}, u32[]{:S(2)}) collective-permute-start(bf16[32,128]{0,1:T(8,128)(2,1)S(1)} %collective-permute-done.3), channel_id=1, source_target_pairs={{0,7},{1,0},{2,1},{3,2},{4,3},{5,4},{6,5},{7,6},{8,15},{9,8},{10,9... | collective-permute-start | bytes 24584 | tf_op jit(solution)/shard_map/ppermute | solution.py:24
  28.5 10.0 %collective-permute-start.7 = (bf16[256,128]{0,1:T(8,128)(2,1)S(1)}, bf16[256,128]{0,1:T(8,128)(2,1)S(1)}, u32[]{:S(2)}, u32[]{:S(2)}) collective-permute-start(bf16[256,128]{0,1:T(8,128)(2,1)S(1)} %dynamic_update_slice.151), channel_id=1, source_target_pairs={{0,8},{8,0},{16,24},{24,16},{32,40},{40,32},{48,56},{56,48},{64,72... | collective-permute-start | bytes 196616 | tf_op jit(solution)/shard_map/ppermute | solution.py:40
  47.2 7.3 %collective-permute-start.13 = (bf16[32,128]{1,0:T(8,128)(2,1)S(1)}, bf16[32,128]{1,0:T(8,128)(2,1)S(1)}, u32[]{:S(2)}, u32[]{:S(2)}) collective-permute-start(bf16[32,128]{1,0:T(8,128)(2,1)S(1)} %collective-permute-done.11), channel_id=1, source_target_pairs={{0,7},{1,0},{2,1},{3,2},{4,3},{5,4},{6,5},{7,6},{8,15},{9,8},{10,9... | collective-permute-start | bytes 24584 | tf_op jit(solution)/shard_map/ppermute | solution.py:24
  71.8 7.3 %collective-permute-start.21 = (bf16[32,128]{1,0:T(8,128)(2,1)S(1)}, bf16[32,128]{1,0:T(8,128)(2,1)S(1)}, u32[]{:S(2)}, u32[]{:S(2)}) collective-permute-start(bf16[32,128]{1,0:T(8,128)(2,1)S(1)} %collective-permute-done.19), channel_id=1, source_target_pairs={{0,7},{1,0},{2,1},{3,2},{4,3},{5,4},{6,5},{7,6},{8,15},{9,8},{10,9... | collective-permute-start | bytes 24584 | tf_op jit(solution)/shard_map/ppermute | solution.py:24
  87.0 8.4 %collective-permute-start.24 = (bf16[512,128]{0,1:T(8,128)(2,1)S(1)}, bf16[512,128]{0,1:T(8,128)(2,1)S(1)}, u32[]{:S(2)}, u32[]{:S(2)}) collective-permute-start(bf16[512,128]{0,1:T(8,128)(2,1)S(1)} %maximum_select_fusion.15), channel_id=1, source_target_pairs={{0,16},{16,0},{8,24},{24,8},{32,48},{48,32},{40,56},{56,40},{64,80... | collective-permute-start | bytes 393224 | tf_op jit(solution)/shard_map/ppermute | solution.py:40
  104.2 7.3 %collective-permute-start.30 = (bf16[32,128]{1,0:T(8,128)(2,1)S(1)}, bf16[32,128]{1,0:T(8,128)(2,1)S(1)}, u32[]{:S(2)}, u32[]{:S(2)}) collective-permute-start(bf16[32,128]{1,0:T(8,128)(2,1)S(1)} %collective-permute-done.28), channel_id=1, source_target_pairs={{0,7},{1,0},{2,1},{3,2},{4,3},{5,4},{6,5},{7,6},{8,15},{9,8},{10,9... | collective-permute-start | bytes 24584 | tf_op jit(solution)/shard_map/ppermute | solution.py:24
  113.1 6.9 %collective-permute-start.32 = (bf16[256,128]{0,1:T(8,128)(2,1)S(1)}, bf16[256,128]{0,1:T(8,128)(2,1)S(1)}, u32[]{:S(2)}, u32[]{:S(2)}) collective-permute-start(bf16[256,128]{0,1:T(8,128)(2,1)S(1)} %dynamic_update_slice.175), channel_id=1, source_target_pairs={{0,8},{8,0},{16,24},{24,16},{32,40},{40,32},{48,56},{56,48},{64,72... | collective-permute-start | bytes 196616 | tf_op jit(solution)/shard_map/ppermute | solution.py:40
  120.0 8.4 %collective-permute-start.33 = (bf16[512,128]{0,1:T(8,128)(2,1)S(1)}, bf16[512,128]{0,1:T(8,128)(2,1)S(1)}, u32[]{:S(2)}, u32[]{:S(2)}) collective-permute-start(bf16[512,128]{0,1:T(8,128)(2,1)S(1)} %maximum_select_fusion.16), channel_id=1, source_target_pairs={{0,16},{16,0},{8,24},{24,8},{32,48},{48,32},{40,56},{56,40},{64,80... | collective-permute-start | bytes 393224 | tf_op jit(solution)/shard_map/ppermute | solution.py:40
  138.0 7.3 %collective-permute-start.39 = (bf16[32,128]{1,0:T(8,128)(2,1)S(1)}, bf16[32,128]{1,0:T(8,128)(2,1)S(1)}, u32[]{:S(2)}, u32[]{:S(2)}) collective-permute-start(bf16[32,128]{1,0:T(8,128)(2,1)S(1)} %collective-permute-done.37), channel_id=1, source_target_pairs={{0,7},{1,0},{2,1},{3,2},{4,3},{5,4},{6,5},{7,6},{8,15},{9,8},{10,9... | collective-permute-start | bytes 24584 | tf_op jit(solution)/shard_map/ppermute | solution.py:24
  153.8 8.4 %collective-permute-start.42 = (bf16[512,128]{0,1:T(8,128)(2,1)S(1)}, bf16[512,128]{0,1:T(8,128)(2,1)S(1)}, u32[]{:S(2)}, u32[]{:S(2)}) collective-permute-start(bf16[512,128]{0,1:T(8,128)(2,1)S(1)} %maximum_select_fusion.17), channel_id=1, source_target_pairs={{0,16},{16,0},{8,24},{24,8},{32,48},{48,32},{40,56},{56,40},{64,80... | collective-permute-start | bytes 393224 | tf_op jit(solution)/shard_map/ppermute | solution.py:40
  162.2 8.3 %collective-permute-start.43 = (bf16[1024,128]{0,1:T(8,128)(2,1)S(1)}, bf16[1024,128]{0,1:T(8,128)(2,1)S(1)}, u32[]{:S(2)}, u32[]{:S(2)}) collective-permute-start(bf16[1024,128]{0,1:T(8,128)(2,1)S(1)} %maximum_select_fusion.9), channel_id=1, source_target_pairs={{0,32},{32,0},{8,40},{40,8},{16,48},{48,16},{24,56},{56,24},{64,96... | collective-permute-start | bytes 786440 | tf_op jit(solution)/shard_map/ppermute | solution.py:40
  179.4 7.3 %collective-permute-start.49 = (bf16[32,128]{1,0:T(8,128)(2,1)S(1)}, bf16[32,128]{1,0:T(8,128)(2,1)S(1)}, u32[]{:S(2)}, u32[]{:S(2)}) collective-permute-start(bf16[32,128]{1,0:T(8,128)(2,1)S(1)} %collective-permute-done.47), channel_id=1, source_target_pairs={{0,7},{1,0},{2,1},{3,2},{4,3},{5,4},{6,5},{7,6},{8,15},{9,8},{10,9... | collective-permute-start | bytes 24584 | tf_op jit(solution)/shard_map/ppermute | solution.py:24
  195.2 8.4 %collective-permute-start.52 = (bf16[512,128]{0,1:T(8,128)(2,1)S(1)}, bf16[512,128]{0,1:T(8,128)(2,1)S(1)}, u32[]{:S(2)}, u32[]{:S(2)}) collective-permute-start(bf16[512,128]{0,1:T(8,128)(2,1)S(1)} %maximum_select_fusion.18), channel_id=1, source_target_pairs={{0,16},{16,0},{8,24},{24,8},{32,48},{48,32},{40,56},{56,40},{64,80... | collective-permute-start | bytes 393224 | tf_op jit(solution)/shard_map/ppermute | solution.py:40
  203.6 8.4 %collective-permute-start.53 = (bf16[1024,128]{0,1:T(8,128)(2,1)S(1)}, bf16[1024,128]{0,1:T(8,128)(2,1)}, u32[]{:S(2)}, u32[]{:S(2)}) collective-permute-start(bf16[1024,128]{0,1:T(8,128)(2,1)S(1)} %maximum_select_fusion.10), channel_id=1, source_target_pairs={{0,32},{32,0},{8,40},{40,8},{16,48},{48,16},{24,56},{56,24},{64,96... | collective-permute-start | bytes 786440 | tf_op jit(solution)/shard_map/ppermute | solution.py:40
  214.0 11.1 %collective-permute-start.54 = (f32[1024,128]{0,1:T(8,128)S(1)}, f32[1024,128]{0,1:T(8,128)S(1)}, u32[]{:S(2)}, u32[]{:S(2)}) collective-permute-start(f32[1024,128]{0,1:T(8,128)S(1)} %slice_select_fusion.1), channel_id=1, source_target_pairs={{0,32},{32,0},{8,40},{40,8},{16,48},{48,16},{24,56},{56,24},{64,96... | collective-permute-start | bytes 1572872 | tf_op jit(solution)/shard_map/ppermute | solution.py:40
  225.3 9.9 %collective-permute-start.55 = (f32[512,128]{0,1:T(8,128)S(1)}, f32[512,128]{0,1:T(8,128)S(1)}, u32[]{:S(2)}, u32[]{:S(2)}) collective-permute-start(f32[512,128]{0,1:T(8,128)S(1)} %slice_select_fusion.5), channel_id=1, source_target_pairs={{0,16},{16,0},{8,24},{24,8},{32,48},{48,32},{40,56},{56,40},{64,80... | collective-permute-start | bytes 786440 | tf_op jit(solution)/shard_map/ppermute | solution.py:40
  235.2 7.7 %collective-permute-start.56 = (f32[256,128]{0,1:T(8,128)S(1)}, f32[256,128]{0,1:T(8,128)S(1)}, u32[]{:S(2)}, u32[]{:S(2)}) collective-permute-start(f32[256,128]{0,1:T(8,128)S(1)} %slice_select_fusion.11), channel_id=1, source_target_pairs={{0,8},{8,0},{16,24},{24,16},{32,40},{40,32},{48,56},{56,48},{64,72... | collective-permute-start | bytes 393224 | tf_op jit(solution)/shard_map/ppermute | solution.py:40
  243.7 115.5 %reduce-scatter.21.cloned.1.call-start = ((), (), s32[]{:S(2)}) async-start(), calls=%async_computation.7 | async-start | bytes 147456 | tf_op jit(solution)/shard_map/reduce_scatter | solution.py:74
  286.8 13.0 %collective-permute-start.57 = (f32[1024,128]{0,1:T(8,128)S(1)}, f32[1024,128]{0,1:T(8,128)S(1)}, u32[]{:S(2)}, u32[]{:S(2)}) collective-permute-start(f32[1024,128]{0,1:T(8,128)S(1)} %slice_select_fusion), channel_id=1, source_target_pairs={{0,32},{32,0},{8,40},{40,8},{16,48},{48,16},{24,56},{56,24},{64,96... | collective-permute-start | bytes 1572872 | tf_op jit(solution)/shard_map/ppermute | solution.py:40
  299.9 9.8 %collective-permute-start.58 = (f32[512,128]{0,1:T(8,128)S(1)}, f32[512,128]{0,1:T(8,128)S(1)}, u32[]{:S(2)}, u32[]{:S(2)}) collective-permute-start(f32[512,128]{0,1:T(8,128)S(1)} %slice_select_fusion.4), channel_id=1, source_target_pairs={{0,16},{16,0},{8,24},{24,8},{32,48},{48,32},{40,56},{56,40},{64,80... | collective-permute-start | bytes 786440 | tf_op jit(solution)/shard_map/ppermute | solution.py:40
  309.8 6.9 %collective-permute-start.59 = (f32[256,128]{0,1:T(8,128)S(1)}, f32[256,128]{0,1:T(8,128)S(1)}, u32[]{:S(2)}, u32[]{:S(2)}) collective-permute-start(f32[256,128]{0,1:T(8,128)S(1)} %slice_select_fusion.10), channel_id=1, source_target_pairs={{0,8},{8,0},{16,24},{24,16},{32,40},{40,32},{48,56},{56,48},{64,72... | collective-permute-start | bytes 393224 | tf_op jit(solution)/shard_map/ppermute | solution.py:40
  317.5 99.9 %reduce-scatter.23.cloned.1.call-start = ((), (), s32[]{:S(2)}) async-start(), calls=%async_computation.8 | async-start | bytes 147456
  360.4 9.8 %collective-permute-start.60 = (f32[512,128]{0,1:T(8,128)S(1)}, f32[512,128]{0,1:T(8,128)S(1)}, u32[]{:S(2)}, u32[]{:S(2)}) collective-permute-start(f32[512,128]{0,1:T(8,128)S(1)} %slice_select_fusion.3), channel_id=1, source_target_pairs={{0,16},{16,0},{8,24},{24,8},{32,48},{48,32},{40,56},{56,40},{64,80... | collective-permute-start | bytes 786440 | tf_op jit(solution)/shard_map/ppermute | solution.py:40
  370.3 6.9 %collective-permute-start.61 = (f32[256,128]{0,1:T(8,128)S(1)}, f32[256,128]{0,1:T(8,128)S(1)}, u32[]{:S(2)}, u32[]{:S(2)}) collective-permute-start(f32[256,128]{0,1:T(8,128)S(1)} %slice_select_fusion.9), channel_id=1, source_target_pairs={{0,8},{8,0},{16,24},{24,16},{32,40},{40,32},{48,56},{56,48},{64,72... | collective-permute-start | bytes 393224 | tf_op jit(solution)/shard_map/ppermute | solution.py:40
  377.9 97.7 %reduce-scatter.25.cloned.1.call-start = ((), (), s32[]{:S(2)}) async-start(), calls=%async_computation.9 | async-start | bytes 147456 | tf_op jit(solution)/shard_map/reduce_scatter | solution.py:74
  418.5 9.9 %collective-permute-start.62 = (f32[512,128]{0,1:T(8,128)S(1)}, f32[512,128]{0,1:T(8,128)S(1)}, u32[]{:S(2)}, u32[]{:S(2)}) collective-permute-start(f32[512,128]{0,1:T(8,128)S(1)} %slice_select_fusion.2), channel_id=1, source_target_pairs={{0,16},{16,0},{8,24},{24,8},{32,48},{48,32},{40,56},{56,40},{64,80... | collective-permute-start | bytes 786440 | tf_op jit(solution)/shard_map/ppermute | solution.py:40
  428.5 6.9 %collective-permute-start.63 = (f32[256,128]{0,1:T(8,128)S(1)}, f32[256,128]{0,1:T(8,128)S(1)}, u32[]{:S(2)}, u32[]{:S(2)}) collective-permute-start(f32[256,128]{0,1:T(8,128)S(1)} %slice_select_fusion.8), channel_id=1, source_target_pairs={{0,8},{8,0},{16,24},{24,16},{32,40},{40,32},{48,56},{56,48},{64,72... | collective-permute-start | bytes 393224 | tf_op jit(solution)/shard_map/ppermute | solution.py:40
  436.2 85.4 %reduce-scatter.27.cloned.1.call-start = ((), (), s32[]{:S(2)}) async-start(), calls=%async_computation.10 | async-start | bytes 147456
  476.6 6.9 %collective-permute-start.64 = (f32[256,128]{0,1:T(8,128)S(1)}, f32[256,128]{0,1:T(8,128)S(1)}, u32[]{:S(2)}, u32[]{:S(2)}) collective-permute-start(f32[256,128]{0,1:T(8,128)S(1)} %slice_select_fusion.7), channel_id=1, source_target_pairs={{0,8},{8,0},{16,24},{24,16},{32,40},{40,32},{48,56},{56,48},{64,72... | collective-permute-start | bytes 393224 | tf_op jit(solution)/shard_map/ppermute | solution.py:40
  484.3 83.6 %reduce-scatter.29.cloned.1.call-start = ((), (), s32[]{:S(2)}) async-start(), calls=%async_computation.11 | async-start | bytes 147456
  522.6 6.9 %collective-permute-start.65 = (f32[256,128]{0,1:T(8,128)S(1)}, f32[256,128]{0,1:T(8,128)S(1)}, u32[]{:S(2)}, u32[]{:S(2)}) collective-permute-start(f32[256,128]{0,1:T(8,128)S(1)} %slice_select_fusion.6), channel_id=1, source_target_pairs={{0,8},{8,0},{16,24},{24,16},{32,40},{40,32},{48,56},{56,48},{64,72... | collective-permute-start | bytes 393224 | tf_op jit(solution)/shard_map/ppermute | solution.py:40
  (49 other events, 557.7 us)
Sparse Core Ops, SparseCore 0:
  243.9 41.6 reduce-scatter.18
  317.6 41.6 reduce-scatter.20
  378.1 39.2 reduce-scatter.22
  436.3 39.2 reduce-scatter.24
  484.4 37.1 reduce-scatter.26
  530.4 37.4 reduce-scatter.28
